TPU v7x, 32 devices: a whole 2x2x4 slice. The times are simulated.
32 devices in a mesh: clips: 2 (over y), frame: 4 (over z), rows: 2 (over x), view: 2 (over core).
Axes of the slice: x: 2, y: 2, z: 4, core: 2. Of those that a mesh axis runs over, the one named last changes fastest.
Arguments:
- feats: bfloat16 [4, 4, 8, 480, 256], P(('clips', 'view'), 'frame', 'rows'), parts along dimension 0, may hold values from -8 to 8
- norm_gains: float32 [3, 256], replicated, may hold values from 0.6 to 10
- cross_qkv: bfloat16 [256, 768], replicated, may hold values from -0.45 to 0.45
- cross_out: bfloat16 [256, 256], replicated, may hold values from -0.375 to 0.375
- time_qkv: bfloat16 [256, 768], replicated, may hold values from -0.45 to 0.45
- time_out: bfloat16 [256, 256], replicated, may hold values from -0.375 to 0.375
- mlp_in: bfloat16 [256, 1024], replicated, may hold values from -0.375 to 0.375
- mlp_out: bfloat16 [1024, 256], replicated, may hold values from -0.1875 to 0.1875
Outputs:
- result: bfloat16 [4, 4, 8, 480, 256], P(('clips', 'view'), 'frame', 'rows'), parts along dimension 0
There are 2 independent parts, one for each index of `clips`. A program takes and returns all parts, laid end to end along the dimension named above; an argument that names none is the same for every part. Nothing has to cross between parts.
All inputs are finite; a program needn't handle non-finite values.
Results may differ from a plain program's by a relative error of at most 0.012.
Values may be sent and summed in bfloat16 or wider, within the bound.
A program may use at most 64 MiB of HBM per device.

v0:
```python
import jax
import jax.numpy as jnp
from jax import lax
from jax.sharding import PartitionSpec as P

HEADS = 8


EPSILON = 1e-05


def swapped(value, axis, bit):
    return lax.ppermute(value, axis, [(i, i ^ 1 << bit) for i in range(lax.axis_size(axis))])


def layer_norm(values, norm_gain):
    wide = values.astype(jnp.float32)
    centre = jnp.mean(wide, axis=-1, keepdims=True)
    spread = jnp.mean((wide - centre) ** 2, axis=-1, keepdims=True)
    return ((wide - centre) * lax.rsqrt(spread + EPSILON) * norm_gain).astype(jnp.bfloat16)


def row_attend(queries, key_rows, value_rows):
    length, channels = queries.shape
    head_dim = channels // HEADS
    q_heads = queries.reshape(length, HEADS, head_dim)
    k_heads = key_rows.reshape(length, HEADS, head_dim)
    v_heads = value_rows.reshape(length, HEADS, head_dim)
    scores = jnp.einsum(
        "qhd,khd->hqk", q_heads, k_heads, preferred_element_type=jnp.float32
    ) * head_dim ** (-0.5)
    top_score = jnp.max(scores, axis=-1, keepdims=True)
    expo = jnp.exp(scores - top_score)
    shares = (expo / jnp.sum(expo, axis=-1, keepdims=True)).astype(jnp.bfloat16)
    mixed = jnp.einsum("hqk,khd->qhd", shares, v_heads, preferred_element_type=jnp.float32)
    return mixed.reshape(length, channels).astype(jnp.bfloat16)


def time_attend(queries, key_rows, value_rows):
    frames, pixels, channels = queries.shape
    head_dim = channels // HEADS
    q_heads = queries.reshape(frames, pixels, HEADS, head_dim)
    k_heads = key_rows.reshape(frames, pixels, HEADS, head_dim)
    v_heads = value_rows.reshape(frames, pixels, HEADS, head_dim)
    scores = jnp.einsum(
        "fnhd,gnhd->hfgn", q_heads, k_heads, preferred_element_type=jnp.float32
    ) * head_dim ** (-0.5)
    top_score = jnp.max(scores, axis=2, keepdims=True)
    expo = jnp.exp(scores - top_score)
    shares = (expo / jnp.sum(expo, axis=2, keepdims=True)).astype(jnp.bfloat16)
    mixed = jnp.einsum("hfgn,gnhd->fnhd", shares, v_heads, preferred_element_type=jnp.float32)
    return mixed.reshape(frames, pixels, channels).astype(jnp.bfloat16)


def local(feats, norm_gains, cross_qkv, cross_out, time_qkv, time_out, mlp_in, mlp_out):
    rows_here, row_width, channels = (feats.shape[2], feats.shape[3], feats.shape[4])
    frame_count = lax.axis_size("frame")
    tokens_flat = feats[0, 0].reshape(-1, channels)
    pixel_count = tokens_flat.shape[0]
    block_pixels = pixel_count // frame_count
    normed_a = layer_norm(tokens_flat, norm_gains[0])
    projected = jnp.dot(normed_a, cross_qkv, preferred_element_type=jnp.float32).astype(
        jnp.bfloat16
    )
    queries = projected[:, :channels]
    partner = swapped(projected[:, channels:], "view", 0)

    def cross_row(pieces):
        return row_attend(pieces[0], pieces[1][:, :channels], pieces[1][:, channels:])

    cross_mix = lax.map(
        cross_row,
        (
            queries.reshape(rows_here, row_width, channels),
            partner.reshape(rows_here, row_width, 2 * channels),
        ),
    )
    cross_mix = cross_mix.reshape(-1, channels)
    stream_b = (
        tokens_flat.astype(jnp.float32)
        + jnp.dot(cross_mix, cross_out, preferred_element_type=jnp.float32)
    ).astype(jnp.bfloat16)
    normed_b = layer_norm(stream_b, norm_gains[1])
    outgoing = normed_b.reshape(1, frame_count, block_pixels, channels)
    gathered = lax.all_to_all(outgoing, "frame", split_axis=1, concat_axis=0, tiled=True)[:, 0]
    frames, pixels, _ = gathered.shape
    projected_b = jnp.dot(
        gathered.reshape(-1, channels), time_qkv, preferred_element_type=jnp.float32
    ).astype(jnp.bfloat16)
    projected_b = projected_b.reshape(frames, pixels, 3 * channels)
    mixed = time_attend(
        projected_b[..., :channels],
        projected_b[..., channels : 2 * channels],
        projected_b[..., 2 * channels :],
    )
    time_mix = mixed[:, None]
    returned = lax.all_to_all(time_mix, "frame", split_axis=0, concat_axis=1, tiled=True).reshape(
        pixel_count, channels
    )
    stream_c = (
        stream_b.astype(jnp.float32)
        + jnp.dot(returned, time_out, preferred_element_type=jnp.float32)
    ).astype(jnp.bfloat16)
    normed_c = layer_norm(stream_c, norm_gains[2])
    inner_act = jax.nn.gelu(
        jnp.dot(normed_c, mlp_in, preferred_element_type=jnp.float32), approximate=True
    ).astype(jnp.bfloat16)
    result = (
        stream_c.astype(jnp.float32)
        + jnp.dot(inner_act, mlp_out, preferred_element_type=jnp.float32)
    ).astype(jnp.bfloat16)
    return result.reshape(1, 1, rows_here, row_width, channels)


def solution(mesh):
    placed = (P(("clips", "view"), "frame", "rows", None, None), P(), P(), P(), P(), P(), P(), P())
    return jax.shard_map(
        local,
        mesh=mesh,
        in_specs=placed,
        out_specs=P(("clips", "view"), "frame", "rows", None, None),
        check_vma=False,
    )
```

profile of v0, /device:TPU:0, one launch (start us, length us, event | category | flops | bytes accessed | tf_op | source)
XLA Modules:
  0.0 185.9 jit_solution(15738146926986763434)
XLA Ops:
  1.7 1.8 multiply_reduce_fusion.1
  4.5 1.8 fusion.42
  10.1 2.8 %collective-permute-done = bf16[1920,512]{1,0:T(8,128)(2,1)S(1)} collective-permute-done((bf16[1920,512]{1,0:T(8,128)(2,1)}, bf16[1920,512]{1,0:T(8,128)(2,1)S(1)}, u32[]{:S(2)}, u32[]{:S(2)}) %collective-permute-start) | collective-permute-done | bytes 1966112 | tf_op jit(solution)/shard_map/ppermute | solution.py:13
  14.3 48.6 %while.10 = (s32[]{:T(128)}, bf16[4,480,256]{2,1,0:T(8,128)(2,1)}, bf16[4,480,512]{2,1,0:T(8,128)(2,1)}, bf16[4,480,256]{2,1,0:T(8,128)(2,1)}, s32[]{:T(128)}) while((s32[]{:T(128)}, bf16[4,480,256]{2,1,0:T(8,128)(2,1)}, bf16[4,480,512]{2,1,0:T(8,128)(2,1)}, bf16[4,480,256]{2,1,0:T(8,128)(2,1)}, s32[]{:T(128)}) %tuple.39), condition=%wide.region_5.6_spmd, body=%wide.region_2.5_spmd.sunk | while | flops 245268960 | bytes 20675140 | solution.py:71
  16.8 4.8 %fusion.91 = (f32[8,480]{1,0:T(8,128)S(1)}, f32[8,480,480]{1,2,0:T(8,128)}) fusion(bf16[480,8,32]{0,2,1:T(8,128)(2,1)S(1)} %bitcast.83, bf16[480,8,32]{0,2,1:T(8,128)(2,1)S(1)} %bitcast.86), kind=kOutput, calls=%fused_computation.73.clone.1 | convolution fusion | flops 123494880 | bytes 7879680 | tf_op jit(solution)/shard_map/while/body/eval_jaxpr/sub | solution.py:33
  21.6 4.0 %fusion.92 = bf16[8,32,480]{2,1,0:T(8,128)(2,1)S(1)} fusion(bf16[480,8,32]{0,2,1:T(8,128)(2,1)S(1)} %bitcast.85, f32[8,480,480]{1,2,0:T(8,128)} %get-tuple-element.101, f32[8,480]{1,0:T(8,128)S(1)} %get-tuple-element.102), kind=kOutput, calls=%fused_computation.7.clone.1 | convolution fusion | flops 121774080 | bytes 7879680 | tf_op jit(solution)/shard_map/while/body/eval_jaxpr/hqk,khd->qhd/dot_general | solution.py:35
  28.9 4.8 %fusion.91 = (f32[8,480]{1,0:T(8,128)S(1)}, f32[8,480,480]{1,2,0:T(8,128)}) fusion(bf16[480,8,32]{0,2,1:T(8,128)(2,1)S(1)} %bitcast.83, bf16[480,8,32]{0,2,1:T(8,128)(2,1)S(1)} %bitcast.86), kind=kOutput, calls=%fused_computation.73.clone.1 | convolution fusion | flops 123494880 | bytes 7879680 | tf_op jit(solution)/shard_map/while/body/eval_jaxpr/sub | solution.py:33
  33.7 4.0 %fusion.92 = bf16[8,32,480]{2,1,0:T(8,128)(2,1)S(1)} fusion(bf16[480,8,32]{0,2,1:T(8,128)(2,1)S(1)} %bitcast.85, f32[8,480,480]{1,2,0:T(8,128)} %get-tuple-element.101, f32[8,480]{1,0:T(8,128)S(1)} %get-tuple-element.102), kind=kOutput, calls=%fused_computation.7.clone.1 | convolution fusion | flops 121774080 | bytes 7879680 | tf_op jit(solution)/shard_map/while/body/eval_jaxpr/hqk,khd->qhd/dot_general | solution.py:35
  41.0 4.8 %fusion.91 = (f32[8,480]{1,0:T(8,128)S(1)}, f32[8,480,480]{1,2,0:T(8,128)}) fusion(bf16[480,8,32]{0,2,1:T(8,128)(2,1)S(1)} %bitcast.83, bf16[480,8,32]{0,2,1:T(8,128)(2,1)S(1)} %bitcast.86), kind=kOutput, calls=%fused_computation.73.clone.1 | convolution fusion | flops 123494880 | bytes 7879680 | tf_op jit(solution)/shard_map/while/body/eval_jaxpr/sub | solution.py:33
  45.8 4.0 %fusion.92 = bf16[8,32,480]{2,1,0:T(8,128)(2,1)S(1)} fusion(bf16[480,8,32]{0,2,1:T(8,128)(2,1)S(1)} %bitcast.85, f32[8,480,480]{1,2,0:T(8,128)} %get-tuple-element.101, f32[8,480]{1,0:T(8,128)S(1)} %get-tuple-element.102), kind=kOutput, calls=%fused_computation.7.clone.1 | convolution fusion | flops 121774080 | bytes 7879680 | tf_op jit(solution)/shard_map/while/body/eval_jaxpr/hqk,khd->qhd/dot_general | solution.py:35
  53.1 4.8 %fusion.91 = (f32[8,480]{1,0:T(8,128)S(1)}, f32[8,480,480]{1,2,0:T(8,128)}) fusion(bf16[480,8,32]{0,2,1:T(8,128)(2,1)S(1)} %bitcast.83, bf16[480,8,32]{0,2,1:T(8,128)(2,1)S(1)} %bitcast.86), kind=kOutput, calls=%fused_computation.73.clone.1 | convolution fusion | flops 123494880 | bytes 7879680 | tf_op jit(solution)/shard_map/while/body/eval_jaxpr/sub | solution.py:33
  57.9 4.0 %fusion.92 = bf16[8,32,480]{2,1,0:T(8,128)(2,1)S(1)} fusion(bf16[480,8,32]{0,2,1:T(8,128)(2,1)S(1)} %bitcast.85, f32[8,480,480]{1,2,0:T(8,128)} %get-tuple-element.101, f32[8,480]{1,0:T(8,128)S(1)} %get-tuple-element.102), kind=kOutput, calls=%fused_computation.7.clone.1 | convolution fusion | flops 121774080 | bytes 7879680 | tf_op jit(solution)/shard_map/while/body/eval_jaxpr/hqk,khd->qhd/dot_general | solution.py:35
  62.8 1.8 convert_reduce_fusion.1
  65.9 30.7 %all_to_all.8 = bf16[1,4,480,256]{3,2,0,1:T(8,128)(2,1)S(1)} all-to-all(bf16[1,4,480,256]{3,2,0,1:T(8,128)(2,1)S(1)} %bitcast.92), channel_id=1, replica_groups=mesh['clips'=2,'frame'=4,'rows'=2,'view'=2] {'frame'}, dimensions={1} | all-to-all | bytes 1966080 | tf_op jit(solution)/shard_map/all_to_all | solution.py:85
  100.5 4.6 %copy.60 = bf16[4,480,8,32]{3,0,1,2:T(4,128)(2,1)} copy(bf16[4,480,8,32]{1,3,2,0:T(8,128)(2,1)S(1)} %bitcast.88) | data formatting | bytes 1966080 | tf_op jit(solution)/shard_map/reshape | solution.py:43
  106.5 4.5 %copy.61 = bf16[4,480,8,32]{3,0,1,2:T(4,128)(2,1)} copy(bf16[4,480,8,32]{1,3,2,0:T(8,128)(2,1)S(1)} %bitcast.89) | data formatting | bytes 1966080 | tf_op jit(solution)/shard_map/reshape | solution.py:42
  111.0 8.4 %fusion.61 = f32[8,480,4,4]{3,2,1,0:T(4,128)} fusion(bf16[4,480,8,32]{3,0,1,2:T(4,128)(2,1)} %copy.60, bf16[4,480,8,32]{3,0,1,2:T(4,128)(2,1)} %copy.61), kind=kOutput, calls=%fused_computation.76 | convolution fusion | flops 3932160 | bytes 2211840 | tf_op jit(solution)/shard_map/fnhd,gnhd->hfgn/dot_general | solution.py:45
  119.4 5.1 %copy.62 = f32[8,480,4,4]{1,0,2,3:T(8,128)S(1)} copy(f32[8,480,4,4]{3,2,1,0:T(4,128)} %fusion.61) | data formatting | bytes 491520 | tf_op jit(solution)/shard_map/fnhd,gnhd->hfgn/dot_general | solution.py:45
  124.7 7.4 %copy.64 = bf16[8,4,4,480]{2,1,0,3:T(4,128)(2,1)} copy(bf16[8,4,4,480]{3,0,2,1:T(8,128)(2,1)S(1)} %divide_convert_fusion.4) | data formatting | bytes 245760 | tf_op jit(solution)/shard_map/convert_element_type | solution.py:50
  132.6 4.7 %copy.63 = bf16[4,480,8,32]{3,0,2,1:T(4,128)(2,1)} copy(bf16[4,480,8,32]{1,3,2,0:T(8,128)(2,1)S(1)} %bitcast.90) | data formatting | bytes 1966080 | tf_op jit(solution)/shard_map/reshape | solution.py:44
  137.3 9.5 %fusion.20 = bf16[4,480,8,32]{3,0,2,1:T(4,128)(2,1)} fusion(bf16[4,480,8,32]{3,0,2,1:T(4,128)(2,1)} %copy.63, bf16[8,4,4,480]{2,1,0,3:T(4,128)(2,1)} %copy.64), kind=kOutput, calls=%fused_computation.24 | convolution fusion | flops 4423680 | bytes 2088960 | tf_op jit(solution)/shard_map/hfgn,gnhd->fnhd/dot_general | solution.py:51
  146.8 5.4 %copy.65 = bf16[4,480,8,32]{1,3,2,0:T(8,128)(2,1)S(1)} copy(bf16[4,480,8,32]{3,0,2,1:T(4,128)(2,1)} %fusion.20) | data formatting | bytes 1966080 | tf_op jit(solution)/shard_map/convert_element_type | solution.py:52
  152.8 26.7 %all_to_all.9 = bf16[4,1,480,256]{3,2,1,0:T(8,128)(2,1)S(1)} all-to-all(bf16[4,1,480,256]{3,2,1,0:T(8,128)(2,1)S(1)} %copy.66), channel_id=1, replica_groups=mesh['clips'=2,'frame'=4,'rows'=2,'view'=2] {'frame'}, dimensions={0} | all-to-all | bytes 1966080 | tf_op jit(solution)/shard_map/all_to_all | solution.py:97
  181.7 4.2 %fusion.27 = bf16[1920,256]{1,0:T(8,128)(2,1)} fusion(bf16[1024,256]{1,0:T(8,128)(2,1)S(1)} %copy-done, bf16[256,1024]{1,0:T(8,128)(2,1)S(1)} %copy-done.6, bf16[1920,256]{1,0:T(8,128)(2,1)S(1)} %get-tuple-element.69, f32[256]{0:T(256)S(1)} %bitcast.98, f32[1920]{0:T(1024)S(1)} %add_rsqrt_fusion, f32[1920]{0:T(1024)S(1)} %broadcast_multiply_fusion), kind=kOutput, calls=%fused_computation.37 | convolution fusion | flops 2034892800 | bytes 3031040 | tf_op jit(solution)/shard_map/dot_general | solution.py:110
  (70 shorter events, 31.0 us)
Async XLA Ops:
  0.0 181.7 %copy-start = (bf16[1024,256]{1,0:T(8,128)(2,1)S(1)}, bf16[1024,256]{1,0:T(8,128)(2,1)}, u32[]{:S(2)}) copy-start(bf16[1024,256]{1,0:T(8,128)(2,1)} %param.17) | copy-start | bytes 1572868
  0.0 6.2 %copy-start.3 = (bf16[256,768]{1,0:T(8,128)(2,1)S(1)}, bf16[256,768]{1,0:T(8,128)(2,1)}, u32[]{:S(2)}) copy-start(bf16[256,768]{1,0:T(8,128)(2,1)} %param.12) | copy-start | bytes 1179652
  8.6 4.3 %collective-permute-start = (bf16[1920,512]{1,0:T(8,128)(2,1)}, bf16[1920,512]{1,0:T(8,128)(2,1)S(1)}, u32[]{:S(2)}, u32[]{:S(2)}) collective-permute-start(bf16[1920,512]{1,0:T(8,128)(2,1)} %slice.40), channel_id=1, source_target_pairs={{0,1},{1,0},{2,3},{3,2},{4,5},{5,4},{6,7},{7,6},{8,9},{9,8},{10,11... | collective-permute-start | bytes 5898248 | tf_op jit(solution)/shard_map/ppermute | solution.py:13
  12.9 1.4 copy-start.2
  14.3 48.6 %copy-start.1 = (bf16[1,1,4,480,256]{4,3,2,1,0:T(8,128)(2,1)S(1)}, bf16[1,1,4,480,256]{4,3,2,1,0:T(8,128)(2,1)}, u32[]{:S(2)}) copy-start(bf16[1,1,4,480,256]{4,3,2,1,0:T(8,128)(2,1)} %param.10) | copy-start | bytes 2949124
  14.3 48.6 %copy-start.5 = (bf16[256,256]{1,0:T(8,128)(2,1)S(1)}, bf16[256,256]{1,0:T(8,128)(2,1)}, u32[]{:S(2)}) copy-start(bf16[256,256]{1,0:T(8,128)(2,1)} %param.13) | copy-start | bytes 393220
  62.8 33.7 %copy-start.4 = (bf16[256,768]{1,0:T(8,128)(2,1)S(1)}, bf16[256,768]{1,0:T(8,128)(2,1)}, u32[]{:S(2)}) copy-start(bf16[256,768]{1,0:T(8,128)(2,1)} %param.14) | copy-start | bytes 1179652
  179.5 2.2 %copy-start.6 = (bf16[256,1024]{1,0:T(8,128)(2,1)S(1)}, bf16[256,1024]{1,0:T(8,128)(2,1)}, u32[]{:S(2)}) copy-start(bf16[256,1024]{1,0:T(8,128)(2,1)} %param.16) | copy-start | bytes 1572868
where the time goes:
time: 187 us; the launch traced here: 186 us
  matrix products  62.5 us (33%)
  blocking collectives  57.4 us (31%)
  local copies, waits for them, and re-layouts  55.2 us (30%)
  other arithmetic  7.24 us (4%)
  waiting for transfers between devices  2.78 us (1%)
    all_to_all x1, blocking collectives, local(): lax.all_to_all(outgoing, 'frame', split_axis=1, concat_axis=0, tiled=True)  30.7 us
    all_to_all x1, blocking collectives, local(): lax.all_to_all(time_mix, 'frame', split_axis=0, concat_axis=1, tiled=True)  26.7 us
    sub x4, matrix products, row_attend(): expo = jnp.exp(scores - top_score)  19.1 us
    dot_general x4, matrix products, row_attend(): jnp.einsum('hqk,khd->qhd', shares, v_heads, preferred_element_type=jnp.fl...  16.1 us
    dynamic_slice x16, local copies, waits for them, and re-layouts, local(): lax.map(cross_row, (queries.reshape(rows_here, row_width, channels), part...  9.61 us
    dot_general x1, matrix products, time_attend(): jnp.einsum('hfgn,gnhd->fnhd', shares, v_heads, preferred_element_type=jnp...  9.5 us
    dot_general x1, matrix products, time_attend(): jnp.einsum('fnhd,gnhd->hfgn', q_heads, k_heads, preferred_element_type=jn...  8.41 us
    convert_element_type x1, local copies, waits for them, and re-layouts, time_attend(): shares = (expo / jnp.sum(expo, axis=2, keepdims=True)).astype(jnp.bfloat16)  7.42 us
  transfers between devices with their start and end apart: 1, of which 1 were waited for; matrix products, arithmetic and copies ran while one was open for 1% of the time, Pallas kernels for 0%

commit v1 on v0

--- a/solution.py
+++ b/solution.py
@@ -1,6 +1,8 @@
 import jax
 import jax.numpy as jnp
 from jax import lax
+from jax.experimental import pallas as pl
+from jax.experimental.pallas import tpu as pltpu
 from jax.sharding import PartitionSpec as P
 
 HEADS = 8
@@ -51,10 +53,235 @@
     mixed = jnp.einsum("hfgn,gnhd->fnhd", shares, v_heads, preferred_element_type=jnp.float32)
     return mixed.reshape(frames, pixels, channels).astype(jnp.bfloat16)
 
+MESH = pl.DeviceIdType.MESH
+LOG2E = 1.4426950408889634
+
+
+def widened_norm(wide, gain):
+    centre = jnp.mean(wide, axis=-1, keepdims=True)
+    moved = wide - centre
+    spread = jnp.mean(moved * moved, axis=-1, keepdims=True)
+    return (moved * lax.rsqrt(spread + EPSILON) * gain).astype(jnp.bfloat16)
+
+
+def head_mask(channels, head_dim, head):
+    lanes = lax.broadcasted_iota(jnp.int32, (1, channels), 1)
+    inside = (lanes >= head * head_dim) & (lanes < (head + 1) * head_dim)
+    return jnp.where(inside, 1.0, 0.0).astype(jnp.bfloat16)
+
+
+def f32_dot(a, b):
+    return jnp.dot(a, b, preferred_element_type=jnp.float32)
+
+
+def block_kernel(
+    feats, gains, cross_qkv, cross_out, time_qkv, time_out, mlp_in, mlp_out,
+    result,
+    other, q_buf, k_buf, v_buf, acc_lo, acc_hi, stream_b, normed_b, arrived, t_proj, mixed, returned,
+    view_send, view_recv, out_send, out_recv, back_send, back_recv,
+):
+    rows, width, channels = feats.shape
+    frames = 4
+    head_dim = channels // HEADS
+    half_heads = HEADS // 2
+    part = width // 2
+    scale = head_dim ** (-0.5) * LOG2E
+    me = lax.axis_index("frame")
+    view = lax.axis_index("view")
+    peers = [lax.rem(me + d, frames) for d in range(1, frames)]
+
+    barrier = pltpu.get_barrier_semaphore()
+    pl.semaphore_signal(barrier, inc=1, device_id={"view": 1 - view}, device_id_type=MESH)
+    for peer in peers:
+        pl.semaphore_signal(barrier, inc=1, device_id={"frame": peer}, device_id_type=MESH)
+    pl.semaphore_wait(barrier, frames)
+
+    def view_copy(row):
+        return pltpu.make_async_remote_copy(
+            src_ref=feats.at[row], dst_ref=other.at[row],
+            send_sem=view_send.at[row], recv_sem=view_recv.at[row],
+            device_id={"view": 1 - view}, device_id_type=MESH)
+
+    def owner_of(row, side):
+        first = 1 - lax.rem((row + 1) // 2, 2)
+        return first if side == 0 else frames - 1 - first
+
+    def out_copy(row, side, turn, source, target):
+        return pltpu.make_async_remote_copy(
+            src_ref=normed_b.at[row, side], dst_ref=arrived.at[turn, source],
+            send_sem=out_send.at[row, side], recv_sem=out_recv.at[turn, source],
+            device_id={"frame": target}, device_id_type=MESH)
+
+    my_side = me // 2
+    my_inner = lax.rem((me + 1) // 2, 2)
+
+    def back_copy(turn, frame, row, side):
+        return pltpu.make_async_remote_copy(
+            src_ref=mixed.at[turn, frame], dst_ref=returned.at[row, side],
+            send_sem=back_send.at[turn, frame], recv_sem=back_recv.at[row, side],
+            device_id={"frame": frame}, device_id_type=MESH)
+
+    for row in range(rows):
+        view_copy(row).start()
+
+    def cross_step(row):
+        own = widened_norm(feats[row].astype(jnp.float32), gains[0:1])
+        q_buf[...] = f32_dot(own, cross_qkv[:, :channels]).astype(jnp.bfloat16)
+        view_copy(row).wait_recv()
+        theirs = widened_norm(other[row].astype(jnp.float32), gains[0:1])
+        k_buf[...] = f32_dot(theirs, cross_qkv[:, channels:2 * channels]).astype(jnp.bfloat16)
+        v_buf[...] = f32_dot(theirs, cross_qkv[:, 2 * channels:]).astype(jnp.bfloat16)
+        acc_lo[...] = jnp.zeros_like(acc_lo)
+        acc_hi[...] = jnp.zeros_like(acc_hi)
+
+        @pl.loop(0, half_heads)
+        def _(head):
+            masks = (head_mask(channels, head_dim, head), head_mask(channels, head_dim, head + half_heads))
+            for low in range(0, width, TILE):
+                for own_head, acc in ((0, acc_lo), (1, acc_hi)):
+                    q_head = q_buf[low:low + TILE] * masks[own_head]
+                    v_head = v_buf[...] * masks[own_head] + masks[1 - own_head]
+                    scores = lax.dot_general(
+                        q_head, k_buf[...], (((1,), (1,)), ((), ())), preferred_element_type=jnp.float32)
+                    top = jnp.max(scores, axis=-1, keepdims=True)
+                    expo = jnp.exp2((scores - top) * scale).astype(jnp.bfloat16)
+                    acc[low:low + TILE] += f32_dot(expo, v_head)
+
+        near = channels // 2
+        mix = jnp.concatenate(
+            [acc_lo[:, :near] / acc_lo[:, near:], acc_hi[:, near:] / acc_hi[:, :near]], axis=1
+        ).astype(jnp.bfloat16)
+        summed = (feats[row].astype(jnp.float32) + f32_dot(mix, cross_out[...])).astype(jnp.bfloat16)
+        stream_b[row] = summed
+        normed = widened_norm(summed.astype(jnp.float32), gains[1:2])
+        turn = row // 2
+        for side in range(2):
+            normed_b[row, side] = normed[side * part:(side + 1) * part]
+            owner = owner_of(row, side)
+
+            @pl.when(owner != me)
+            def _():
+                out_copy(row, side, turn, me, owner).start()
+
+            @pl.when(owner == me)
+            def _():
+                arrived[turn, me] = normed_b[row, side]
+
+    def time_step(turn):
+        for peer in peers:
+            out_copy(0, 0, turn, peer, peer).wait_recv()
+        for frame in range(frames):
+            t_proj[frame] = f32_dot(arrived[turn, frame], time_qkv[...]).astype(jnp.bfloat16)
+        down_c = lax.broadcasted_iota(jnp.int32, (channels, 128), 0)
+        down_h = lax.broadcasted_iota(jnp.int32, (channels, 128), 1)
+        gather = jnp.where(
+            (down_c >= down_h * head_dim) & (down_c < (down_h + 1) * head_dim), 1.0, 0.0
+        ).astype(jnp.bfloat16)
+        up_h = lax.broadcasted_iota(jnp.int32, (128, channels), 0)
+        up_c = lax.broadcasted_iota(jnp.int32, (128, channels), 1)
+        spread = jnp.where(
+            (up_c >= up_h * head_dim) & (up_c < (up_h + 1) * head_dim), 1.0, 0.0
+        ).astype(jnp.bfloat16)
+
+        @pl.loop(0, part // PIX)
+        def _(block):
+            span = pl.ds(pl.multiple_of(block * PIX, PIX), PIX)
+            for frame in range(frames):
+                query = t_proj[frame, span, :channels].astype(jnp.float32)
+                scores = []
+                for other_frame in range(frames):
+                    product = query * t_proj[other_frame, span, channels:2 * channels].astype(jnp.float32)
+                    high = product.astype(jnp.bfloat16)
+                    low = (product - high.astype(jnp.float32)).astype(jnp.bfloat16)
+                    scores.append(f32_dot(high, gather) + f32_dot(low, gather))
+                top = jnp.maximum(jnp.maximum(scores[0], scores[1]), jnp.maximum(scores[2], scores[3]))
+                expo = [jnp.exp2((s - top) * scale) for s in scores]
+                total = 1.0 / (expo[0] + expo[1] + expo[2] + expo[3])
+                mix = jnp.zeros((PIX, channels), jnp.float32)
+                for other_frame in range(frames):
+                    share = f32_dot((expo[other_frame] * total).astype(jnp.bfloat16), spread)
+                    mix = mix + share * t_proj[other_frame, span, 2 * channels:].astype(jnp.float32)
+                mixed[turn, frame, span] = mix.astype(jnp.bfloat16)
+
+        row = 2 * turn + lax.rem(turn + 1 + my_inner, 2)
+        for peer in peers:
+            back_copy(turn, peer, row, my_side).start()
+        returned[row, my_side] = mixed[turn, me]
+
+    def mlp_step(row):
+        for side in range(2):
+            @pl.when(owner_of(row, side) != me)
+            def _():
+                back_copy(0, me, row, side).wait_recv()
+
+            sl = slice(side * part, (side + 1) * part)
+            summed = (
+                stream_b[row, sl].astype(jnp.float32) + f32_dot(returned[row, side], time_out[...])
+            ).astype(jnp.bfloat16)
+            wide = summed.astype(jnp.float32)
+            normed = widened_norm(wide, gains[2:3])
+            act = jax.nn.gelu(f32_dot(normed, mlp_in[...]), approximate=True).astype(jnp.bfloat16)
+            result[row, sl] = (wide + f32_dot(act, mlp_out[...])).astype(jnp.bfloat16)
+
+    pl.loop(0, rows)(cross_step)
+    pl.loop(0, 2)(time_step)
+    pl.loop(0, rows)(mlp_step)
+
+    @pl.loop(0, rows)
+    def _(row):
+        view_copy(row).wait_send()
+        for side in range(2):
+            @pl.when(owner_of(row, side) != me)
+            def _():
+                out_copy(row, side, 0, me, me).wait_send()
+
+    for turn in range(2):
+        for peer in peers:
+            back_copy(turn, peer, 0, 0).wait_send()
+
+
+TILE = 240
+PIX = 48
+
+
+def fused(feats, norm_gains, cross_qkv, cross_out, time_qkv, time_out, mlp_in, mlp_out):
+    rows, width, channels = feats.shape[2:]
+    part = width // 2
+    bf16, f32 = jnp.bfloat16, jnp.float32
+    dma = pltpu.SemaphoreType.DMA
+    return pl.pallas_call(
+        block_kernel,
+        out_shape=jax.ShapeDtypeStruct((rows, width, channels), bf16),
+        in_specs=[pl.BlockSpec(memory_space=pltpu.VMEM)] * 8,
+        out_specs=pl.BlockSpec(memory_space=pltpu.VMEM),
+        scratch_shapes=[
+            pltpu.VMEM((rows, width, channels), bf16),
+            pltpu.VMEM((width, channels), bf16),
+            pltpu.VMEM((width, channels), bf16),
+            pltpu.VMEM((width, channels), bf16),
+            pltpu.VMEM((width, channels), f32),
+            pltpu.VMEM((width, channels), f32),
+            pltpu.VMEM((rows, width, channels), bf16),
+            pltpu.VMEM((rows, 2, part, channels), bf16),
+            pltpu.VMEM((2, 4, part, channels), bf16),
+            pltpu.VMEM((4, part, 3 * channels), bf16),
+            pltpu.VMEM((2, 4, part, channels), bf16),
+            pltpu.VMEM((rows, 2, part, channels), bf16),
+            dma((rows,)), dma((rows,)),
+            dma((rows, 2)), dma((2, 4)),
+            dma((2, 4)), dma((rows, 2)),
+        ],
+        compiler_params=pltpu.CompilerParams(
+            collective_id=0, has_side_effects=True, vmem_limit_bytes=56 * 1024 * 1024),
+        name="stereo_block",
+    )(feats[0, 0], norm_gains, cross_qkv, cross_out, time_qkv, time_out, mlp_in, mlp_out)[None, None]
+
 
 def local(feats, norm_gains, cross_qkv, cross_out, time_qkv, time_out, mlp_in, mlp_out):
     rows_here, row_width, channels = (feats.shape[2], feats.shape[3], feats.shape[4])
     frame_count = lax.axis_size("frame")
+    if frame_count == 4 and rows_here == 4 and row_width == 2 * TILE and channels == 256:
+        return fused(feats, norm_gains, cross_qkv, cross_out, time_qkv, time_out, mlp_in, mlp_out)
     tokens_flat = feats[0, 0].reshape(-1, channels)
     pixel_count = tokens_flat.shape[0]
     block_pixels = pixel_count // frame_count

time: 187 us -> 61.7 us (0.33)
  the two profiles are of different devices: /device:TPU:0 before, /device:TPU:24 now
where the time goes in v1:
time: 61.7 us; the launch traced here: 61.5 us
  Pallas kernels  59.3 us (96%)
  local copies, waits for them, and re-layouts  2.21 us (4%)
    pallas_call x1, Pallas kernels, fused(): pl.pallas_call(block_kernel, out_shape=jax.ShapeDtypeStruct((rows, width,...  59.3 us
    unnamed x1, local copies, waits for them, and re-layouts  2.21 us

profile of v1, /device:TPU:24, one launch (start us, length us, event | category | flops | bytes accessed | tf_op | source)
XLA Modules:
  0.0 61.5 jit_solution(14186190133867883389)
XLA Ops:
  0.0 59.3 %stereo_block.1 = bf16[4,480,256]{2,1,0:T(8,128)(2,1)} custom-call(bf16[4,480,256]{2,1,0:T(8,128)(2,1)} %bitcast.3, f32[3,256]{1,0:T(4,128)} %gains.1, bf16[256,768]{1,0:T(8,128)(2,1)} %cross_qkv.1, bf16[256,256]{1,0:T(8,128)(2,1)} %cross_out.1, bf16[256,768]{1,0:T(8,128)(2,1)} %time_qkv.1, bf16[256,256]{1,0:T(8,128)(2,1)} %time_out.1, ...), custom_call_target="tpu_custom_call" | custom-call | tf_op jit(solution)/shard_map/stereo_block/pallas_call | solution.py:252
  59.3 2.2 %copy.10 = bf16[1,1,4,480,256]{4,3,2,1,0:T(8,128)(2,1)} copy(bf16[1,1,4,480,256]{4,3,2,1,0:T(8,128)(2,1)} %bitcast.2) | data formatting | bytes 1966080

commit v2 on v1

--- a/solution.py
+++ b/solution.py
@@ -134,7 +134,7 @@
         acc_lo[...] = jnp.zeros_like(acc_lo)
         acc_hi[...] = jnp.zeros_like(acc_hi)
 
-        @pl.loop(0, half_heads)
+        @pl.loop(0, half_heads, unroll=UNROLL)
         def _(head):
             masks = (head_mask(channels, head_dim, head), head_mask(channels, head_dim, head + half_heads))
             for low in range(0, width, TILE):
@@ -188,19 +188,22 @@
             span = pl.ds(pl.multiple_of(block * PIX, PIX), PIX)
             for frame in range(frames):
                 query = t_proj[frame, span, :channels].astype(jnp.float32)
-                scores = []
-                for other_frame in range(frames):
-                    product = query * t_proj[other_frame, span, channels:2 * channels].astype(jnp.float32)
-                    high = product.astype(jnp.bfloat16)
-                    low = (product - high.astype(jnp.float32)).astype(jnp.bfloat16)
-                    scores.append(f32_dot(high, gather) + f32_dot(low, gather))
+                product = jnp.concatenate(
+                    [query * t_proj[g, span, channels:2 * channels].astype(jnp.float32) for g in range(frames)],
+                    axis=0)
+                high = product.astype(jnp.bfloat16)
+                low = (product - high.astype(jnp.float32)).astype(jnp.bfloat16)
+                stacked = f32_dot(high, gather) + f32_dot(low, gather)
+                scores = [stacked[g * PIX:(g + 1) * PIX] for g in range(frames)]
                 top = jnp.maximum(jnp.maximum(scores[0], scores[1]), jnp.maximum(scores[2], scores[3]))
                 expo = [jnp.exp2((s - top) * scale) for s in scores]
                 total = 1.0 / (expo[0] + expo[1] + expo[2] + expo[3])
+                shares = jnp.concatenate([e * total for e in expo], axis=0).astype(jnp.bfloat16)
+                wide_shares = f32_dot(shares, spread)
                 mix = jnp.zeros((PIX, channels), jnp.float32)
-                for other_frame in range(frames):
-                    share = f32_dot((expo[other_frame] * total).astype(jnp.bfloat16), spread)
-                    mix = mix + share * t_proj[other_frame, span, 2 * channels:].astype(jnp.float32)
+                for g in range(frames):
+                    mix = mix + wide_shares[g * PIX:(g + 1) * PIX] * t_proj[
+                        g, span, 2 * channels:].astype(jnp.float32)
                 mixed[turn, frame, span] = mix.astype(jnp.bfloat16)
 
         row = 2 * turn + lax.rem(turn + 1 + my_inner, 2)
@@ -240,8 +243,9 @@
             back_copy(turn, peer, 0, 0).wait_send()
 
 
-TILE = 240
-PIX = 48
+UNROLL = 4
+TILE = 480
+PIX = 240
 
 
 def fused(feats, norm_gains, cross_qkv, cross_out, time_qkv, time_out, mlp_in, mlp_out):
@@ -280,7 +284,7 @@
 def local(feats, norm_gains, cross_qkv, cross_out, time_qkv, time_out, mlp_in, mlp_out):
     rows_here, row_width, channels = (feats.shape[2], feats.shape[3], feats.shape[4])
     frame_count = lax.axis_size("frame")
-    if frame_count == 4 and rows_here == 4 and row_width == 2 * TILE and channels == 256:
+    if frame_count == 4 and rows_here == 4 and row_width == 480 and channels == 256:
         return fused(feats, norm_gains, cross_qkv, cross_out, time_qkv, time_out, mlp_in, mlp_out)
     tokens_flat = feats[0, 0].reshape(-1, channels)
     pixel_count = tokens_flat.shape[0]

time: 61.7 us -> 59.3 us (0.961)
  Pallas kernels: 59.3 us -> 56.7 us
    pallas_call x1, Pallas kernels: 59.3 us -> 56.7 us  [fused(): pl.pallas_call(block_kernel, out_shape=jax.ShapeDtypeStruct((rows, width,...]
where the time goes in v2:
time: 59.3 us; the launch traced here: 58.9 us
  Pallas kernels  56.7 us (96%)
  local copies, waits for them, and re-layouts  2.21 us (4%)
    pallas_call x1, Pallas kernels, fused(): pl.pallas_call(block_kernel, out_shape=jax.ShapeDtypeStruct((rows, width,...  56.7 us
    unnamed x1, local copies, waits for them, and re-layouts  2.21 us

profile of v2, /device:TPU:24, one launch (start us, length us, event | category | flops | bytes accessed | tf_op | source)
XLA Modules:
  0.0 58.9 jit_solution(12106649576027340428)
XLA Ops:
  0.0 56.7 %stereo_block.1 = bf16[4,480,256]{2,1,0:T(8,128)(2,1)} custom-call(bf16[4,480,256]{2,1,0:T(8,128)(2,1)} %bitcast.3, f32[3,256]{1,0:T(4,128)} %gains.1, bf16[256,768]{1,0:T(8,128)(2,1)} %cross_qkv.1, bf16[256,256]{1,0:T(8,128)(2,1)} %cross_out.1, bf16[256,768]{1,0:T(8,128)(2,1)} %time_qkv.1, bf16[256,256]{1,0:T(8,128)(2,1)} %time_out.1, ...), custom_call_target="tpu_custom_call" | custom-call | tf_op jit(solution)/shard_map/stereo_block/pallas_call | solution.py:256
  56.7 2.2 %copy.10 = bf16[1,1,4,480,256]{4,3,2,1,0:T(8,128)(2,1)} copy(bf16[1,1,4,480,256]{4,3,2,1,0:T(8,128)(2,1)} %bitcast.2) | data formatting | bytes 1966080
